TPU v7x, 32 devices: a whole 2x2x4 slice. The times are simulated.
32 devices in a mesh: groups: 2 (over x), sector: 16 (over z, y, core).
Axes of the slice: x: 2, y: 2, z: 4, core: 2. Of those that a mesh axis runs over, the one named last changes fastest.
Arguments:
- wavefunction: bfloat16 [256, 4, 128, 128], P(('groups', 'sector')), parts along dimension 0, may hold values from -46 to 46
- left_env: bfloat16 [16, 256, 128, 128], P(None, ('groups', 'sector')), parts along dimension 1, may hold values from -2 to 2
- right_env: bfloat16 [16, 256, 128, 128], P(None, ('groups', 'sector')), parts along dimension 1, may hold values from -2 to 2
- energy_diag: float32 [256, 4, 128, 128], P(('groups', 'sector')), parts along dimension 0, may hold values from -1 to 1.5
- sector_dims: int32 [2, 128], replicated, may hold values from 32 to 128
- pair_table: int32 [128, 4], replicated, may hold values from 0 to 127, as said below
Outputs:
- sigma_blocks: bfloat16 [256, 4, 128, 128], P(('groups', 'sector')), parts along dimension 0
- correction: float32 [256, 4, 128, 128], P(('groups', 'sector')), parts along dimension 0
There are 2 independent parts, one for each index of `groups`. A program takes and returns all parts, laid end to end along the dimension named above; an argument that names none is the same for every part. Nothing has to cross between parts.
Inputs may be any that keep to these rules, and one draw needn't show every extreme that they name: `pair_table`: right sector b is held by index b // 8 of sector. The 4 right sectors of one left sector are distinct. Among the blocks of the 8 left sectors of one index of sector, at most 4 have right sectors held by any one index; in every draw some index of sector holds the right sectors of exactly 4 blocks from every index.
All inputs are finite; a program needn't handle non-finite values.
Results may differ from a plain program's by a relative error of at most 0.0068.
Values may be sent and summed in bfloat16 or wider, within the bound.
A program may use at most 256 MiB of HBM per device.

v0:
```python
import jax
import jax.numpy as jnp
from jax import lax
from jax.sharding import PartitionSpec as P


def body(wavefunction, left_env, right_env, energy_diag, sector_dims, pair_table):
    local_sectors = wavefunction.shape[0]
    partners = wavefunction.shape[1]
    tile_size = wavefunction.shape[2]
    term_count = left_env.shape[0]
    peer_count = lax.axis_size("sector")
    my_index = lax.axis_index("sector")
    blocks = local_sectors * partners
    slot_cap = 2 * -(-blocks // peer_count)
    slot_total = peer_count * slot_cap
    first_row = my_index * local_sectors
    my_pairs = lax.dynamic_slice_in_dim(pair_table, first_row, local_sectors, 0)
    left_dims = lax.dynamic_slice_in_dim(sector_dims[0], first_row, local_sectors, 0)
    right_dims = jnp.take(sector_dims[1], my_pairs)
    positions = jnp.arange(tile_size, dtype=jnp.int32)
    live_mask = (
        (positions[None, None, :, None] < left_dims[:, None, None, None])
        & (positions[None, None, None, :] < right_dims[:, :, None, None])
    ).astype(jnp.bfloat16)
    masked = wavefunction * live_mask
    partial_blocks = jnp.einsum(
        "wsij,skjl->wskil", left_env, masked, preferred_element_type=jnp.float32
    )
    partial_blocks = partial_blocks.astype(jnp.bfloat16).reshape(
        term_count, blocks, tile_size, tile_size
    )
    owner_all = (pair_table // local_sectors).reshape(peer_count, blocks)
    peer_ids = jnp.arange(peer_count, dtype=jnp.int32)
    matches = (owner_all[:, :, None] == peer_ids[None, None, :]).astype(jnp.int32)
    earlier = jnp.cumsum(matches, axis=1) - matches
    rank_all = jnp.sum(earlier * matches, axis=2)
    my_owner = lax.dynamic_index_in_dim(owner_all, my_index, 0, keepdims=False)
    my_rank = lax.dynamic_index_in_dim(rank_all, my_index, 0, keepdims=False)
    my_slot = my_owner * slot_cap + my_rank
    slot_ranks = jnp.arange(slot_cap, dtype=jnp.int32)
    incoming = (
        (owner_all == my_index)[:, None, :] & (rank_all[:, None, :] == slot_ranks[None, :, None])
    ).astype(jnp.int32)
    flat_pairs = pair_table.reshape(peer_count, blocks)
    incoming_live = jnp.sum(incoming, axis=2)
    right_local = (
        jnp.sum(incoming * flat_pairs[:, None, :], axis=2) - first_row * incoming_live
    ).reshape(slot_total)
    slot_ids = jnp.arange(slot_total, dtype=jnp.int32)
    slot_pick = (my_slot[None, :] == slot_ids[:, None]).astype(jnp.int32)
    source_block = jnp.sum(slot_pick * jnp.arange(blocks, dtype=jnp.int32)[None, :], axis=1)
    slot_live = jnp.sum(slot_pick, axis=1).astype(jnp.bfloat16)
    outgoing = jnp.take(partial_blocks, source_block, axis=1) * slot_live[None, :, None, None]
    outgoing = outgoing.reshape(term_count, peer_count, slot_cap, tile_size, tile_size)
    arrived = lax.all_to_all(outgoing, "sector", split_axis=1, concat_axis=1, tiled=True)
    arrived = arrived.reshape(term_count, slot_total, tile_size, tile_size)
    gathered_right = jnp.take(right_env, right_local, axis=1)
    slot_sums = jnp.einsum(
        "wsil,wsml->sim", arrived, gathered_right, preferred_element_type=jnp.float32
    )
    slot_sums = slot_sums.astype(jnp.bfloat16).reshape(peer_count, slot_cap, tile_size, tile_size)
    returned = lax.all_to_all(slot_sums, "sector", split_axis=0, concat_axis=0, tiled=True)
    summed = jnp.take(returned.reshape(slot_total, tile_size, tile_size), my_slot, axis=0)
    sigma_blocks = summed.reshape(local_sectors, partners, tile_size, tile_size) * live_mask
    masked_wide = masked.astype(jnp.float32)
    sigma_wide = sigma_blocks.astype(jnp.float32)
    correlation, norm_sum = lax.psum(
        (jnp.sum(masked_wide * sigma_wide), jnp.sum(masked_wide * masked_wide)), "sector"
    )
    quotient = correlation / norm_sum
    residual = sigma_wide - quotient * masked_wide
    distance = quotient - energy_diag
    correction = residual * distance / (distance * distance + 0.25)
    return (sigma_blocks, correction)


def solution(mesh):
    placed = (
        P(("groups", "sector"), None, None, None),
        P(None, ("groups", "sector"), None, None),
        P(None, ("groups", "sector"), None, None),
        P(("groups", "sector"), None, None, None),
        P(),
        P(),
    )
    return jax.shard_map(
        body,
        mesh=mesh,
        in_specs=placed,
        out_specs=(
            P(("groups", "sector"), None, None, None),
            P(("groups", "sector"), None, None, None),
        ),
        check_vma=False,
    )
```

profile of v0, /device:TPU:0, one launch (start us, length us, event | category | flops | bytes accessed | tf_op | source)
XLA Modules:
  0.0 948.6 jit_solution(4218776534995803640)
XLA Ops:
  0.6 0.9 copy.38
  1.5 0.7 add_select_fusion
  2.2 0.1 copy.39
  2.3 0.1 reshape.195
  2.5 0.1 mul.103
  2.6 0.1 reshape.202
  2.7 0.8 fusion.25
  3.4 0.7 gather_fusion
  4.1 0.1 reshape.201
  4.5 0.8 fusion.26
  5.4 0.2 convert_reduce_fusion
  5.6 0.1 copy.47
  5.7 0.1 sub.39
  5.8 0.2 add_reduce_fusion
  6.0 0.1 convert_reduce_fusion.1
  6.1 0.1 reduce_sum.69
  6.2 10.4 %convolution_convert_fusion = bf16[8,4,128,16,128]{4,2,3,1,0:T(8,128)(2,1)} fusion(bf16[8,4,128,128]{3,2,1,0:T(8,128)(2,1)S(1)} %copy-done, pred[8,4,128]{2,1,0:T(4,128)(4,1)S(1)} %iota_compare_fusion.4, pred[8,128]{1,0:T(8,128)(4,1)S(1)} %iota_compare_fusion.5, bf16[16,8,128,128]{3,2,1,0:T(8,128)(2,1)} %param.7), kind=kOutput, calls=%fused_computation.10 | convolution fusion | flops 2156920832 | bytes 22025216 | tf_op jit(solution)/shard_map/wsij,skjl->wskil/dot_general | solution.py:27
  16.6 18.0 %gather_fusion.1 = bf16[64,16,128,128]{2,3,1,0:T(8,128)(2,1)} fusion(bf16[16,32,128,128]{2,3,0,1:T(8,128)(2,1)} %bitcast.42, s32[1024]{0:T(1024)S(1)} %pad_clamp_fusion.2), kind=kCustom, calls=%fused_computation.1 | custom fusion | bytes 67109120 | tf_op jit(solution)/shard_map/jit(_take)/gather | solution.py:54
  34.6 42.0 %copy.44 = bf16[16,16,4,128,128]{4,3,0,2,1:T(8,128)(2,1)} copy(bf16[16,16,4,128,128]{3,4,0,2,1:T(8,128)(2,1)} %bitcast.43) | data formatting | bytes 67108864 | tf_op jit(solution)/shard_map/jit(_take)/gather | solution.py:54
  76.6 0.1 convert_element_type.40
  76.7 22.8 %select_multiply_fusion = bf16[16,16,4,128,128]{4,3,0,2,1:T(8,128)(2,1)} fusion(bf16[16,16,4,128,128]{4,3,0,2,1:T(8,128)(2,1)} %copy.44, pred[16,4]{1,0:T(8,128)(4,1)S(1)} %compare_and_fusion, bf16[16,4]{1,0:T(8,128)(2,1)S(1)} %convert_element_type.40), kind=kLoop, calls=%fused_computation.7 | loop fusion | flops 33554432 | bytes 67109056 | tf_op jit(solution)/shard_map/mul | solution.py:54
  99.6 7.4 all-to-all-start
  107.0 0.1 sub.38
  107.1 14.3 %gather_fusion.2 = bf16[64,16,128,128]{3,2,1,0:T(8,128)(2,1)} fusion(bf16[16,8,128,128]{3,2,1,0:T(8,128)(2,1)} %param.8, s32[1024]{0:T(1024)S(1)} %pad_clamp_fusion.1), kind=kCustom, calls=%fused_computation.2 | custom fusion | bytes 67109120 | tf_op jit(solution)/shard_map/jit(_take)/gather | solution.py:58
  121.4 574.5 %all-to-all-done = bf16[16,16,4,128,128]{4,3,0,2,1:T(8,128)(2,1)} async-done(((bf16[16,16,4,128,128]{4,3,0,2,1:T(8,128)(2,1)}), bf16[16,16,4,128,128]{4,3,0,2,1:T(8,128)(2,1)}, u32[]{:S(2)}, u32[]{:S(2)}) %all-to-all-start) | async-done | bytes 33554464 | tf_op jit(solution)/shard_map/all_to_all | solution.py:56
  695.9 24.4 %bitcast_convert_fusion = bf16[64,128,128]{2,1,0:T(8,128)(2,1)} fusion(bf16[16,64,128,128]{3,2,0,1:T(8,128)(2,1)} %bitcast.10, bf16[64,16,128,128]{3,2,1,0:T(8,128)(2,1)} %gather_fusion.2, pred[64]{0:T(512)(128)(4,1)S(1)} %compare_and_fusion.2), kind=kOutput, calls=%fused_computation.11 | convolution fusion | flops 4312793088 | bytes 69206080 | tf_op jit(solution)/shard_map/wsil,wsml->sim/dot_general | solution.py:59
  720.3 137.6 %all-to-all-start.1 = ((bf16[16,4,128,128]{3,2,1,0:T(8,128)(2,1)}), bf16[16,4,128,128]{3,2,1,0:T(8,128)(2,1)S(1)}, u32[]{:S(2)}, u32[]{:S(2)}) async-start(bf16[16,4,128,128]{3,2,1,0:T(8,128)(2,1)} %bitcast.46), calls=%async_computation.1 | async-start | bytes 4194304 | tf_op jit(solution)/shard_map/all_to_all | solution.py:63
  858.0 41.0 %all-to-all-done.1 = bf16[16,4,128,128]{3,2,1,0:T(8,128)(2,1)S(1)} async-done(((bf16[16,4,128,128]{3,2,1,0:T(8,128)(2,1)}), bf16[16,4,128,128]{3,2,1,0:T(8,128)(2,1)S(1)}, u32[]{:S(2)}, u32[]{:S(2)}) %all-to-all-start.1) | async-done | bytes 2097184 | tf_op jit(solution)/shard_map/all_to_all | solution.py:63
  899.0 1.6 gather_fusion.3
  900.7 2.9 fusion.11
  903.6 39.8 %all-reduce = (f32[]{:T(128)}, f32[]{:T(128)}) all-reduce(f32[]{:T(128)} %get-tuple-element.3, f32[]{:T(128)} %get-tuple-element.2), channel_id=1, replica_groups=mesh['groups'=2,'sector'=16] {'sector'}, use_global_device_ids=true, to_apply=%region_7.8 | all-reduce | flops 2 | bytes 16 | tf_op jit(solution)/shard_map/psum | solution.py:68
  944.7 4.0 fusion.9
  (24 shorter events, 0.6 us)
Async XLA Ops:
  0.6 5.6 copy-start
  99.6 596.3 %all-to-all-start = ((bf16[16,16,4,128,128]{4,3,0,2,1:T(8,128)(2,1)}), bf16[16,16,4,128,128]{4,3,0,2,1:T(8,128)(2,1)}, u32[]{:S(2)}, u32[]{:S(2)}) async-start(bf16[16,16,4,128,128]{4,3,0,2,1:T(8,128)(2,1)} %select_multiply_fusion), calls=%async_computation | async-start | bytes 67108864 | tf_op jit(solution)/shard_map/all_to_all | solution.py:56
  720.3 178.7 %all-to-all-start.1 = ((bf16[16,4,128,128]{3,2,1,0:T(8,128)(2,1)}), bf16[16,4,128,128]{3,2,1,0:T(8,128)(2,1)S(1)}, u32[]{:S(2)}, u32[]{:S(2)}) async-start(bf16[16,4,128,128]{3,2,1,0:T(8,128)(2,1)} %bitcast.46), calls=%async_computation.1 | async-start | bytes 4194304 | tf_op jit(solution)/shard_map/all_to_all | solution.py:63
  903.6 45.0 %copy-start.1 = (bf16[8,4,128,128]{3,2,1,0:T(8,128)(2,1)}, bf16[8,4,128,128]{3,2,1,0:T(8,128)(2,1)S(1)}, u32[]{:S(2)}) copy-start(bf16[8,4,128,128]{3,2,1,0:T(8,128)(2,1)S(1)} %get-tuple-element.10) | copy-start | bytes 3145732
where the time goes:
time: 950 us; the launch traced here: 949 us
  waiting for transfers between devices  615 us (65%)
  starting transfers between devices  145 us (15%)
  local copies, waits for them, and re-layouts  79.5 us (8%)
  blocking collectives  39.8 us (4%)
  matrix products  34.8 us (4%)
  other arithmetic  32 us (3%)
    all_to_all x1, waiting for transfers between devices, body(): lax.all_to_all(outgoing, 'sector', split_axis=1, concat_axis=1, tiled=True)  574 us
    all_to_all x1, starting transfers between devices, body(): lax.all_to_all(slot_sums, 'sector', split_axis=0, concat_axis=0, tiled=True)  138 us
    gather x2, local copies, waits for them, and re-layouts, body(): jnp.take(partial_blocks, source_block, axis=1)  60 us
    all_to_all x1, waiting for transfers between devices, body(): lax.all_to_all(slot_sums, 'sector', split_axis=0, concat_axis=0, tiled=True)  41 us
    psum x1, blocking collectives, body(): lax.psum((jnp.sum(masked_wide * sigma_wide), jnp.sum(masked_wide * masked...  39.8 us
    dot_general x1, matrix products, body(): jnp.einsum('wsil,wsml->sim', arrived, gathered_right, preferred_element_t...  24.4 us
    mul x1, other arithmetic, body(): jnp.take(partial_blocks, source_block, axis=1)  22.8 us
  transfers between devices with their start and end apart: 2, of which 2 were waited for; matrix products, arithmetic and copies ran while one was open for 2% of the time, Pallas kernels for 0%

commit v1 on v0

v1 whole, which is shorter than its diff:
```python
import functools
import jax
import jax.numpy as jnp
from jax import lax
from jax.experimental import pallas as pl
from jax.experimental.pallas import tpu as pltpu
from jax.sharding import PartitionSpec as P

TEAM = 4
PARTS = 2


def exchange_kernel(lines, terms, left_ref, right_ref, wave_ref, left_all, right_all, wave_all,
                    team_send, team_recv, side_send, side_recv, line_send, line_recv, local_sem):
    me = lax.axis_index("sector")
    line = me // TEAM
    member = me % TEAM
    half = terms // PARTS
    pieces = TEAM * PARTS

    def peer(x):
        return ((member // 2 + x // 2) % 2) * 2 + (member % 2 + x % 2) % 2

    barrier = pltpu.get_barrier_semaphore()

    def greet(who):
        pl.semaphore_signal(barrier, inc=1, device_id={"sector": who},
                            device_id_type=pl.DeviceIdType.MESH)

    for x in range(1, TEAM):
        greet(line * TEAM + peer(x))

    @pl.when(line > 0)
    def _():
        greet(me - TEAM)

    @pl.when(line < lines - 1)
    def _():
        greet(me + TEAM)

    ends = (line == 0).astype(jnp.int32) + (line == lines - 1).astype(jnp.int32)
    pl.semaphore_wait(barrier, TEAM + 1 - ends)

    def remote(src, dst, send, recv, who):
        return pltpu.make_async_remote_copy(
            src_ref=src, dst_ref=dst, send_sem=send, recv_sem=recv,
            device_id={"sector": who}, device_id_type=pl.DeviceIdType.MESH)

    def team_copy(x, part):
        q = x * PARTS + part
        other = peer(x)
        return remote(right_ref.at[pl.ds(other * terms + part * half, half)],
                      right_all.at[me, pl.ds(part * half, half)],
                      team_send.at[q], team_recv.at[q], line * TEAM + other)

    def left_copy(x):
        other = peer(x)
        return remote(left_ref.at[pl.ds(other * terms, terms)], left_all.at[member],
                      side_send.at[0, x], side_recv.at[0, x], line * TEAM + other)

    def wave_copy(x):
        other = peer(x)
        return remote(wave_ref, wave_all.at[member],
                      side_send.at[1, x], side_recv.at[1, x], line * TEAM + other)

    def line_copy(up, hop, q):
        x, part = q // PARTS, q % PARTS
        step = 1 if up else -1
        origin = (line - step * (hop - 1)) * TEAM + peer(x)
        there = right_all.at[origin, pl.ds(part * half, half)]
        if hop == 1 and x == 0:
            src = right_ref.at[pl.ds(member * terms + part * half, half)]
        else:
            src = there
        side = 0 if up else 1
        return remote(src, there, line_send.at[side, hop - 1, q],
                      line_recv.at[side, hop - 1, q], me + step * TEAM)

    def can_send(up, hop):
        if up:
            return (line >= hop - 1) & (line < lines - 1)
        return (line + hop - 1 < lines) & (line > 0)

    keep = [
        pltpu.make_async_copy(right_ref.at[pl.ds(member * terms, terms)], right_all.at[me], local_sem.at[0]),
        pltpu.make_async_copy(left_ref.at[pl.ds(member * terms, terms)], left_all.at[member], local_sem.at[1]),
        pltpu.make_async_copy(wave_ref, wave_all.at[member], local_sem.at[2]),
    ]
    for q in range(PARTS, pieces):
        team_copy(q // PARTS, q % PARTS).start()
    for slot in range(pieces + lines - 2):
        for hop in range(1, lines):
            q = slot - (hop - 1)
            if not 0 <= q < pieces:
                continue
            if hop == 1 and q >= PARTS:
                team_copy(q // PARTS, q % PARTS).wait_recv()
            for up in (True, False):
                @pl.when(can_send(up, hop))
                def _():
                    if hop > 1:
                        line_copy(up, hop - 1, q).wait_recv()
                    line_copy(up, hop, q).start()
        if slot == PARTS - 1:
            for copy in keep:
                copy.start()
            for x in range(1, TEAM):
                left_copy(x).start()
                wave_copy(x).start()
    for q in range(pieces):
        for hop in range(1, lines):
            for up in (True, False):
                end = lines - 1 if up else 0
                from_there = (line >= hop) if up else (line + hop < lines)

                @pl.when((line == end) & from_there)
                def _():
                    line_copy(up, hop, q).wait_recv()

                @pl.when(can_send(up, hop))
                def _():
                    line_copy(up, hop, q).wait_send()
    for q in range(PARTS, pieces):
        team_copy(q // PARTS, q % PARTS).wait_send()
    for x in range(1, TEAM):
        left_copy(x).wait()
        wave_copy(x).wait()
    for copy in keep:
        copy.wait()


def exchange(wave, left_env, right_env, peer_count):
    total, sectors, size, _ = left_env.shape
    terms = total // TEAM
    lines = peer_count // TEAM
    pieces = TEAM * PARTS
    dma = pltpu.SemaphoreType.DMA
    hbm = pl.BlockSpec(memory_space=pl.ANY)
    return pl.pallas_call(
        functools.partial(exchange_kernel, lines, terms),
        out_shape=(
            jax.ShapeDtypeStruct((TEAM, terms, sectors, size, size), left_env.dtype),
            jax.ShapeDtypeStruct((peer_count, terms, sectors, size, size), right_env.dtype),
            jax.ShapeDtypeStruct((TEAM,) + wave.shape, wave.dtype),
        ),
        in_specs=[hbm] * 3,
        out_specs=(hbm, hbm, hbm),
        scratch_shapes=[
            dma((pieces,)), dma((pieces,)),
            dma((2, TEAM)), dma((2, TEAM)),
            dma((2, lines - 1, pieces)), dma((2, lines - 1, pieces)),
            dma((3,)),
        ],
        compiler_params=pltpu.CompilerParams(collective_id=0, has_side_effects=True),
        name="exchange",
    )(left_env, right_env, wave)


def products_kernel(partners, terms, pairs_ref, rows_ref, cols_ref, left_ref, wave_ref, *rest):
    right_refs, out_ref = rest[:partners], rest[partners]
    size = wave_ref.shape[-1]
    step = pl.program_id(0)
    row_ids = lax.broadcasted_iota(jnp.int32, (size, size), 0)
    col_ids = lax.broadcasted_iota(jnp.int32, (size, size), 1)
    masked = []
    for k in range(partners):
        live = (row_ids < rows_ref[step]) & (col_ids < cols_ref[step * partners + k])
        masked.append(jnp.where(live, wave_ref[0, 0, k], jnp.zeros((), wave_ref.dtype)))
    masked = jnp.concatenate(masked, axis=1)
    halves = [jnp.dot(left_ref[0, w, 0], masked, preferred_element_type=jnp.float32).astype(jnp.bfloat16)
              for w in range(terms)]
    for k in range(partners):
        first = jnp.concatenate([p[:, k * size:(k + 1) * size] for p in halves], axis=1)
        second = jnp.concatenate([right_refs[k][0, w, 0] for w in range(terms)], axis=1)
        out_ref[0, 0, k] = lax.dot_general(
            first, second, (((1,), (1,)), ((), ())), preferred_element_type=jnp.float32
        ).astype(out_ref.dtype)


def products(pairs, rows, cols, left_all, right_all, wave_all):
    team, sectors, partners, size, _ = wave_all.shape
    terms = left_all.shape[1]

    def pick(k):
        def index(i, pairs_ref, rows_ref, cols_ref):
            b = pairs_ref[i * partners + k]
            return (b // sectors, 0, b % sectors, 0, 0)
        return pl.BlockSpec((1, terms, 1, size, size), index)

    def own(i, *_):
        return (i // sectors, i % sectors, 0, 0, 0)

    blocks = team * sectors * partners
    return pl.pallas_call(
        functools.partial(products_kernel, partners, terms),
        grid_spec=pltpu.PrefetchScalarGridSpec(
            num_scalar_prefetch=3,
            grid=(team * sectors,),
            in_specs=[
                pl.BlockSpec((1, terms, 1, size, size), lambda i, *_: (i // sectors, 0, i % sectors, 0, 0)),
                pl.BlockSpec((1, 1, partners, size, size), own),
            ] + [pick(k) for k in range(partners)],
            out_specs=pl.BlockSpec((1, 1, partners, size, size), own),
        ),
        out_shape=jax.ShapeDtypeStruct(wave_all.shape, jnp.bfloat16),
        compiler_params=pltpu.CompilerParams(vmem_limit_bytes=32 * 1024 * 1024),
        cost_estimate=pl.CostEstimate(flops=4 * blocks * terms * size ** 3,
                                      bytes_accessed=28 * 2 ** 20, transcendentals=0),
        name="products",
    )(pairs, rows, cols, left_all, wave_all, *([right_all] * partners))


def body(wavefunction, left_env, right_env, energy_diag, sector_dims, pair_table):
    local_sectors = wavefunction.shape[0]
    tile_size = wavefunction.shape[2]
    peer_count = lax.axis_size("sector")
    my_index = lax.axis_index("sector")
    line = my_index // TEAM
    team_sectors = TEAM * local_sectors
    team_first = line * team_sectors
    team_pairs = lax.dynamic_slice_in_dim(pair_table, team_first, team_sectors, 0)
    team_rows = lax.dynamic_slice_in_dim(sector_dims[0], team_first, team_sectors, 0)
    team_cols = jnp.take(sector_dims[1], team_pairs)
    left_all, right_all, wave_all = exchange(wavefunction, left_env, right_env, peer_count)
    sums = products(team_pairs.reshape(-1), team_rows, team_cols.reshape(-1), left_all, right_all, wave_all)
    teams = [[g * TEAM + i for i in range(TEAM)] for g in range(peer_count // TEAM)]
    arrived = lax.all_to_all(sums, "sector", split_axis=0, concat_axis=0, axis_index_groups=teams, tiled=True)
    summed = jnp.sum(arrived.astype(jnp.float32), axis=0)
    member_first = (my_index % TEAM) * local_sectors
    left_dims = lax.dynamic_slice_in_dim(team_rows, member_first, local_sectors, 0)
    right_dims = lax.dynamic_slice_in_dim(team_cols, member_first, local_sectors, 0)
    positions = jnp.arange(tile_size, dtype=jnp.int32)
    live = (positions[None, None, :, None] < left_dims[:, None, None, None]) & (
        positions[None, None, None, :] < right_dims[:, :, None, None])
    masked_wide = jnp.where(live, wavefunction.astype(jnp.float32), 0.0)
    sigma_blocks = jnp.where(live, summed, 0.0).astype(jnp.bfloat16)
    sigma_wide = sigma_blocks.astype(jnp.float32)
    correlation, norm_sum = lax.psum(
        (jnp.sum(masked_wide * sigma_wide), jnp.sum(masked_wide * masked_wide)), "sector")
    quotient = correlation / norm_sum
    residual = sigma_wide - quotient * masked_wide
    distance = quotient - energy_diag
    correction = residual * distance / (distance * distance + 0.25)
    return (sigma_blocks, correction)


def solution(mesh):
    blocks = P(("groups", "sector"), None, None, None)
    environments = P(None, ("groups", "sector"), None, None)
    return jax.shard_map(
        body,
        mesh=mesh,
        in_specs=(blocks, environments, environments, blocks, P(), P()),
        out_specs=(blocks, blocks),
        check_vma=False,
    )
```

time: 950 us -> 412 us (0.43)
  waiting for transfers between devices: 615 us -> 48 us
  Pallas kernels: 0 us -> 306 us
  starting transfers between devices: 145 us -> 4.85 us
  local copies, waits for them, and re-layouts: 79.5 us -> 9.69 us
  matrix products: 34.8 us -> 0 us
  other arithmetic: 32 us -> 8.61 us
    all_to_all x2 -> x1, waiting for transfers between devices: 615 us -> 48 us  [body(): lax.all_to_all(sums, 'sector', split_axis=0, concat_axis=0, axis_index_gr...]
    pallas_call x0 -> x2, Pallas kernels: none -> 306 us  [the longest x1 277 us: exchange(): pl.pallas_call(functools.partial(exchange_kernel, lines, terms), out_shap...]
    all_to_all x2 -> x1, starting transfers between devices: 145 us -> 4.85 us  [body(): lax.all_to_all(sums, 'sector', split_axis=0, concat_axis=0, axis_index_gr...]
    gather x6 -> x2, local copies, waits for them, and re-layouts: 76.8 us -> 1.32 us  [body(): team_cols = jnp.take(sector_dims[1], team_pairs)]
    dot_general x2 -> x0, matrix products: 34.8 us -> none  [the longest x1 24.4 us: body(): jnp.einsum('wsil,wsml->sim', arrived, gathered_right, preferred_element_t...]
    mul x1 -> x0, other arithmetic: 22.8 us -> none  [body(): jnp.take(partial_blocks, source_block, axis=1)]
  transfers between devices with their start and end apart: 2 -> 1, of which waited for: 2 -> 1; matrix products, arithmetic and copies ran while one was open for 2% -> 0% of each run, Pallas kernels for 0% -> 0%
where the time goes in v1:
time: 412 us; the launch traced here: 411 us
  Pallas kernels  306 us (74%)
  waiting for transfers between devices  48 us (12%)
  blocking collectives  31.9 us (8%)
  local copies, waits for them, and re-layouts  9.69 us (2%)
  other arithmetic  8.61 us (2%)
  starting transfers between devices  4.85 us (1%)
    pallas_call x1, Pallas kernels, exchange(): pl.pallas_call(functools.partial(exchange_kernel, lines, terms), out_shap...  277 us
    all_to_all x1, waiting for transfers between devices, body(): lax.all_to_all(sums, 'sector', split_axis=0, concat_axis=0, axis_index_gr...  48 us
    psum x1, blocking collectives, body(): lax.psum((jnp.sum(masked_wide * sigma_wide), jnp.sum(masked_wide * masked...  31.9 us
    pallas_call x1, Pallas kernels, products(): pl.pallas_call(functools.partial(products_kernel, partners, terms), grid_...  29.2 us
  transfers between devices with their start and end apart: 1, of which 1 were waited for; matrix products, arithmetic and copies ran while one was open for 0% of the time, Pallas kernels for 0%

profile of v1, /device:TPU:0, one launch (start us, length us, event | category | flops | bytes accessed | tf_op | source)
XLA Modules:
  0.0 411.1 jit_solution(7967946538293238488)
XLA Ops:
  0.6 0.0 copy-start
  0.7 0.7 copy-done
  1.3 0.1 constant_dynamic-slice_fusion.2
  1.4 0.1 copy.10
  1.5 0.1 reshape.56.pairs_ref
  1.6 0.8 fusion.7
  2.4 0.1 fusion.5.rows_ref
  2.4 0.1 reshape.59
  2.5 1.2 gather_fusion
  3.8 0.1 reshape.58
  3.9 0.1 select_n.51.cols_ref
  4.0 276.8 %exchange.1 = (bf16[4,4,8,128,128]{4,3,2,1,0:T(8,128)(2,1)}, bf16[16,4,8,128,128]{4,3,2,1,0:T(8,128)(2,1)}, bf16[4,8,4,128,128]{4,3,2,1,0:T(8,128)(2,1)}) custom-call(bf16[16,8,128,128]{3,2,1,0:T(8,128)(2,1)} %left_ref.1, bf16[16,8,128,128]{3,2,1,0:T(8,128)(2,1)} %right_ref.1, bf16[8,4,128,128]{3,2,1,0:T(8,128)(2,1)} %wave_ref.1), custom_call_target="tpu_custom_call" | custom-call | tf_op jit(solution)/shard_map/exchange/pallas_call | solution.py:139
  280.8 0.0 copy-start.2
  280.8 2.2 copy-done.2
  283.0 0.0 copy-start.3
  283.0 2.2 copy-done.3
  285.2 29.2 %products.1 = bf16[4,8,4,128,128]{4,3,2,1,0:T(8,128)(2,1)S(1)} custom-call(s32[128]{0:T(128)S(1)} %reshape.56.pairs_ref, s32[32]{0:T(128)S(1)} %fusion.5.rows_ref, s32[128]{0:T(128)S(1)} %select_n.51.cols_ref, bf16[4,4,8,128,128]{4,3,2,1,0:T(8,128)(2,1)S(1)} %copy-done.2, bf16[4,8,4,128,128]{4,3,2,1,0:T(8,128)(2,1)S(1)} %copy-done.3, ...), custom_call_target="tpu_custom_call" | custom-call | flops 4294967296 | bytes 29360128 | tf_op jit(solution)/shard_map/products/pallas_call | solution.py:194
  314.4 0.0 copy-start.1
  314.4 2.0 copy-done.1
  316.4 4.9 %all-to-all-start = ((bf16[4,8,4,128,128]{4,3,2,1,0:T(8,128)(2,1)}), bf16[4,8,4,128,128]{4,3,2,1,0:T(8,128)(2,1)}, u32[]{:S(2)}, u32[]{:S(2)}) async-start(bf16[4,8,4,128,128]{4,3,2,1,0:T(8,128)(2,1)} %copy-done.1), calls=%async_computation | async-start | bytes 8388608 | tf_op jit(solution)/shard_map/all_to_all | solution.py:227
  321.2 0.1 fusion.4
  321.3 0.1 iota_compare_fusion.1
  321.4 0.1 iota_compare_fusion
  321.5 0.0 copy-start.4
  321.5 48.0 %all-to-all-done = bf16[4,8,4,128,128]{4,3,2,1,0:T(8,128)(2,1)} async-done(((bf16[4,8,4,128,128]{4,3,2,1,0:T(8,128)(2,1)}), bf16[4,8,4,128,128]{4,3,2,1,0:T(8,128)(2,1)}, u32[]{:S(2)}, u32[]{:S(2)}) %all-to-all-start) | async-done | bytes 4194336 | tf_op jit(solution)/shard_map/all_to_all | solution.py:227
  369.4 3.0 convert_reduce_fusion
  372.5 0.0 copy-done.4
  372.5 1.5 multiply_reduce_fusion
  374.0 0.0 copy-start.5
  374.0 31.9 %all-reduce = (f32[]{:T(128)}, f32[]{:T(128)}) all-reduce(f32[]{:T(128)} %get-tuple-element.9, f32[]{:T(128)} %get-tuple-element.8), channel_id=1, replica_groups=mesh['groups'=2,'sector'=16] {'sector'}, use_global_device_ids=true, to_apply=%region_2.3 | all-reduce | flops 2 | bytes 16 | tf_op jit(solution)/shard_map/psum | solution.py:238
  407.2 3.9 fusion.2
  411.1 0.0 copy-done.5
  (4 shorter events, 0.0 us)
Async XLA Ops:
  0.6 0.7 copy-start
  280.8 2.2 copy-start.2
  283.0 2.2 copy-start.3
  314.4 2.0 copy-start.1
  316.4 53.1 %all-to-all-start = ((bf16[4,8,4,128,128]{4,3,2,1,0:T(8,128)(2,1)}), bf16[4,8,4,128,128]{4,3,2,1,0:T(8,128)(2,1)}, u32[]{:S(2)}, u32[]{:S(2)}) async-start(bf16[4,8,4,128,128]{4,3,2,1,0:T(8,128)(2,1)} %copy-done.1), calls=%async_computation | async-start | bytes 8388608 | tf_op jit(solution)/shard_map/all_to_all | solution.py:227
  321.5 51.0 %copy-start.4 = (bf16[8,4,128,128]{3,2,1,0:T(8,128)(2,1)S(1)}, bf16[8,4,128,128]{3,2,1,0:T(8,128)(2,1)}, u32[]{:S(2)}) copy-start(bf16[8,4,128,128]{3,2,1,0:T(8,128)(2,1)} %wave_ref.1) | copy-start | bytes 3145732
  374.0 37.1 %copy-start.5 = (bf16[8,4,128,128]{3,2,1,0:T(8,128)(2,1)}, bf16[8,4,128,128]{3,2,1,0:T(8,128)(2,1)S(1)}, u32[]{:S(2)}) copy-start(bf16[8,4,128,128]{3,2,1,0:T(8,128)(2,1)S(1)} %get-tuple-element.12) | copy-start | bytes 3145732

commit v2 on v1

--- a/solution.py
+++ b/solution.py
@@ -202,7 +202,7 @@
             ] + [pick(k) for k in range(partners)],
             out_specs=pl.BlockSpec((1, 1, partners, size, size), own),
         ),
-        out_shape=jax.ShapeDtypeStruct(wave_all.shape, jnp.bfloat16),
+        out_shape=jax.ShapeDtypeStruct(wave_all.shape, jnp.float32),
         compiler_params=pltpu.CompilerParams(vmem_limit_bytes=32 * 1024 * 1024),
         cost_estimate=pl.CostEstimate(flops=4 * blocks * terms * size ** 3,
                                       bytes_accessed=28 * 2 ** 20, transcendentals=0),
@@ -210,9 +210,148 @@
     )(pairs, rows, cols, left_all, wave_all, *([right_all] * partners))
 
 
+def finish_kernel(peers, rows_ref, cols_ref, sums_ref, wave_ref, energy_ref, sigma_ref, correction_ref,
+                  far_own, far_in, far_out, near_own, near_in, cross_in, mine, gathered,
+                  load_sem, near_send, near_recv, far_send, far_recv, cross_send, cross_recv, stat_send, stat_recv):
+    sectors, partners, size, _ = wave_ref.shape
+    me = lax.axis_index("sector")
+    line = me // TEAM
+    member = me % TEAM
+    row, core = member // 2, member % 2
+    near = line * TEAM + row * 2 + 1 - core
+    cross = line * TEAM + (1 - row) * 2 + core
+
+    barrier = pltpu.get_barrier_semaphore()
+
+    @pl.loop(1, peers)
+    def _(d):
+        pl.semaphore_signal(barrier, inc=1, device_id={"sector": lax.rem(me + d, peers)},
+                            device_id_type=pl.DeviceIdType.MESH)
+
+    pl.semaphore_wait(barrier, peers - 1)
+
+    def remote(src, dst, send, recv, who):
+        return pltpu.make_async_remote_copy(
+            src_ref=src, dst_ref=dst, send_sem=send, recv_sem=recv,
+            device_id={"sector": who}, device_id_type=pl.DeviceIdType.MESH)
+
+    def far_copy(i):
+        return remote(sums_ref.at[(1 - row) * 2 + 1 - core, i], far_in.at[i], far_send.at[i], far_recv.at[i], near)
+
+    def near_copy(i):
+        return remote(sums_ref.at[row * 2 + 1 - core, i], near_in.at[i], near_send.at[i], near_recv.at[i], near)
+
+    def cross_copy(i):
+        return remote(far_out.at[i], cross_in.at[i], cross_send.at[i], cross_recv.at[i], cross)
+
+    def stat_copy(d):
+        return remote(mine, gathered.at[me], stat_send.at[d], stat_recv.at[d], lax.rem(me + d, peers))
+
+    load_far = pltpu.make_async_copy(sums_ref.at[(1 - row) * 2 + core], far_own, load_sem.at[0])
+    load_near = pltpu.make_async_copy(sums_ref.at[member], near_own, load_sem.at[1])
+    load_far.start()
+
+    @pl.loop(0, sectors)
+    def _(i):
+        far_copy(i).start()
+
+    load_near.start()
+
+    @pl.loop(0, sectors)
+    def _(i):
+        near_copy(i).start()
+
+    load_far.wait()
+
+    @pl.loop(0, sectors)
+    def _(i):
+        far_copy(i).wait_recv()
+        far_out[i] = (far_own[i] + far_in[i]).astype(far_out.dtype)
+        cross_copy(i).start()
+
+    load_near.wait()
+    row_ids = lax.broadcasted_iota(jnp.int32, (size, size), 0)
+    col_ids = lax.broadcasted_iota(jnp.int32, (size, size), 1)
+
+    def fold(x):
+        return jnp.sum(x.reshape(size // 8, 8, size), axis=0)
+
+    mine[...] = jnp.zeros_like(mine)
+
+    @pl.loop(0, sectors)
+    def _(i):
+        near_copy(i).wait_recv()
+        cross_copy(i).wait_recv()
+        for k in range(partners):
+            live = (row_ids < rows_ref[i]) & (col_ids < cols_ref[i * partners + k])
+            masked = jnp.where(live, wave_ref[i, k].astype(jnp.float32), 0.0)
+            total = near_own[i, k] + near_in[i, k] + cross_in[i, k].astype(jnp.float32)
+            sigma = jnp.where(live, total, 0.0).astype(jnp.bfloat16)
+            sigma_ref[i, k] = sigma
+            mine[0:8] += fold(masked * sigma.astype(jnp.float32))
+            mine[8:16] += fold(masked * masked)
+
+    @pl.loop(1, peers)
+    def _(d):
+        stat_copy(d).start()
+
+    gathered[me] = mine[...]
+
+    @pl.loop(0, sectors)
+    def _(i):
+        far_copy(i).wait_send()
+        near_copy(i).wait_send()
+        cross_copy(i).wait_send()
+
+    @pl.loop(1, peers)
+    def _(d):
+        stat_copy(d).wait()
+
+    both = jnp.sum(gathered[...], axis=0)
+    correlation = jnp.sum(jnp.sum(both[0:8], axis=0, keepdims=True), axis=1, keepdims=True)
+    norm_sum = jnp.sum(jnp.sum(both[8:16], axis=0, keepdims=True), axis=1, keepdims=True)
+    quotient = correlation / norm_sum
+
+    @pl.loop(0, sectors)
+    def _(i):
+        for k in range(partners):
+            live = (row_ids < rows_ref[i]) & (col_ids < cols_ref[i * partners + k])
+            masked = jnp.where(live, wave_ref[i, k].astype(jnp.float32), 0.0)
+            residual = sigma_ref[i, k].astype(jnp.float32) - quotient * masked
+            distance = quotient - energy_ref[i, k]
+            correction_ref[i, k] = residual * distance / (distance * distance + 0.25)
+
+
+def finish(rows, cols, sums, wave, energy, peers):
+    sectors, partners, size, _ = wave.shape
+    dma = pltpu.SemaphoreType.DMA
+    smem = pl.BlockSpec(memory_space=pltpu.SMEM)
+    vmem = pl.BlockSpec(memory_space=pltpu.VMEM)
+    return pl.pallas_call(
+        functools.partial(finish_kernel, peers),
+        out_shape=(
+            jax.ShapeDtypeStruct(wave.shape, jnp.bfloat16),
+            jax.ShapeDtypeStruct(wave.shape, jnp.float32),
+        ),
+        in_specs=[smem, smem, pl.BlockSpec(memory_space=pl.ANY), vmem, vmem],
+        out_specs=(vmem, vmem),
+        scratch_shapes=[
+            pltpu.VMEM(wave.shape, jnp.float32), pltpu.VMEM(wave.shape, jnp.float32),
+            pltpu.VMEM(wave.shape, jnp.bfloat16),
+            pltpu.VMEM(wave.shape, jnp.float32), pltpu.VMEM(wave.shape, jnp.float32),
+            pltpu.VMEM(wave.shape, jnp.bfloat16),
+            pltpu.VMEM((16, size), jnp.float32), pltpu.VMEM((peers, 16, size), jnp.float32),
+            dma((2,)), dma((sectors,)), dma((sectors,)), dma((sectors,)), dma((sectors,)),
+            dma((sectors,)), dma((sectors,)), dma((peers,)), dma((peers,)),
+        ],
+        compiler_params=pltpu.CompilerParams(collective_id=1, has_side_effects=True,
+                                             vmem_limit_bytes=40 * 1024 * 1024),
+        name="finish",
+    )(rows, cols, sums, wave, energy)
+
+
 def body(wavefunction, left_env, right_env, energy_diag, sector_dims, pair_table):
     local_sectors = wavefunction.shape[0]
-    tile_size = wavefunction.shape[2]
     peer_count = lax.axis_size("sector")
     my_index = lax.axis_index("sector")
     line = my_index // TEAM
@@ -223,25 +362,10 @@
     team_cols = jnp.take(sector_dims[1], team_pairs)
     left_all, right_all, wave_all = exchange(wavefunction, left_env, right_env, peer_count)
     sums = products(team_pairs.reshape(-1), team_rows, team_cols.reshape(-1), left_all, right_all, wave_all)
-    teams = [[g * TEAM + i for i in range(TEAM)] for g in range(peer_count // TEAM)]
-    arrived = lax.all_to_all(sums, "sector", split_axis=0, concat_axis=0, axis_index_groups=teams, tiled=True)
-    summed = jnp.sum(arrived.astype(jnp.float32), axis=0)
     member_first = (my_index % TEAM) * local_sectors
-    left_dims = lax.dynamic_slice_in_dim(team_rows, member_first, local_sectors, 0)
-    right_dims = lax.dynamic_slice_in_dim(team_cols, member_first, local_sectors, 0)
-    positions = jnp.arange(tile_size, dtype=jnp.int32)
-    live = (positions[None, None, :, None] < left_dims[:, None, None, None]) & (
-        positions[None, None, None, :] < right_dims[:, :, None, None])
-    masked_wide = jnp.where(live, wavefunction.astype(jnp.float32), 0.0)
-    sigma_blocks = jnp.where(live, summed, 0.0).astype(jnp.bfloat16)
-    sigma_wide = sigma_blocks.astype(jnp.float32)
-    correlation, norm_sum = lax.psum(
-        (jnp.sum(masked_wide * sigma_wide), jnp.sum(masked_wide * masked_wide)), "sector")
-    quotient = correlation / norm_sum
-    residual = sigma_wide - quotient * masked_wide
-    distance = quotient - energy_diag
-    correction = residual * distance / (distance * distance + 0.25)
-    return (sigma_blocks, correction)
+    rows = lax.dynamic_slice_in_dim(team_rows, member_first, local_sectors, 0)
+    cols = lax.dynamic_slice_in_dim(team_cols, member_first, local_sectors, 0)
+    return finish(rows, cols.reshape(-1), sums, wavefunction, energy_diag, peer_count)
 
 
 def solution(mesh):

time: 412 us -> 356 us (0.86)
  waiting for transfers between devices: 48 us -> 0 us
  Pallas kernels: 306 us -> 341 us
  blocking collectives: 31.9 us -> 0 us
  other arithmetic: 8.61 us -> 0.02 us
  starting transfers between devices: 4.85 us -> 0 us
    all_to_all x1 -> x0, waiting for transfers between devices: 48 us -> none  [body(): lax.all_to_all(sums, 'sector', split_axis=0, concat_axis=0, axis_index_gr...]
    pallas_call x0 -> x1, Pallas kernels: none -> 35.3 us  [finish(): pl.pallas_call(functools.partial(finish_kernel, peers), out_shape=(jax.Sh...]
    psum x1 -> x0, blocking collectives: 31.9 us -> none  [body(): lax.psum((jnp.sum(masked_wide * sigma_wide), jnp.sum(masked_wide * masked...]
    all_to_all x1 -> x0, starting transfers between devices: 4.85 us -> none  [body(): lax.all_to_all(sums, 'sector', split_axis=0, concat_axis=0, axis_index_gr...]
    reduce_sum x2 -> x0, other arithmetic: 4.5 us -> none  [the longest x1 3 us: body(): summed = jnp.sum(arrived.astype(jnp.float32), axis=0)]
    unnamed x13 -> x15, local copies, waits for them, and re-layouts: 7.08 us -> 9.99 us
  transfers between devices with their start and end apart: 1 -> 0, of which waited for: 1 -> 0; matrix products, arithmetic and copies ran while one was open for 0% -> 0% of each run, Pallas kernels for 0% -> 0%
where the time goes in v2:
time: 356 us; the launch traced here: 355 us
  Pallas kernels  341 us (96%)
  local copies, waits for them, and re-layouts  12.7 us (4%)
    pallas_call x1, Pallas kernels, exchange(): pl.pallas_call(functools.partial(exchange_kernel, lines, terms), out_shap...  277 us
    pallas_call x1, Pallas kernels, finish(): pl.pallas_call(functools.partial(finish_kernel, peers), out_shape=(jax.Sh...  35.3 us
    pallas_call x1, Pallas kernels, products(): pl.pallas_call(functools.partial(products_kernel, partners, terms), grid_...  29.4 us
    unnamed x15, local copies, waits for them, and re-layouts  9.99 us

profile of v2, /device:TPU:0, one launch (start us, length us, event | category | flops | bytes accessed | tf_op | source)
XLA Modules:
  0.0 354.9 jit_solution(11043341533374353269)
XLA Ops:
  0.6 0.0 copy-start
  0.7 0.8 slice_bitcast_fusion
  1.4 0.1 fusion.rows_ref
  1.5 0.1 fusion.1.rows_ref
  1.6 0.0 copy-done
  1.6 0.1 constant_dynamic-slice_fusion.2
  1.7 0.1 copy.10
  1.8 0.1 reshape.24.pairs_ref
  1.9 0.1 reshape.27
  2.0 1.2 gather_fusion
  3.2 0.1 reshape.26
  3.3 0.1 select_n.44.cols_ref
  3.5 0.1 reshape.23.cols_ref
  3.5 276.8 %exchange.1 = (bf16[4,4,8,128,128]{4,3,2,1,0:T(8,128)(2,1)}, bf16[16,4,8,128,128]{4,3,2,1,0:T(8,128)(2,1)}, bf16[4,8,4,128,128]{4,3,2,1,0:T(8,128)(2,1)}) custom-call(bf16[16,8,128,128]{3,2,1,0:T(8,128)(2,1)} %left_ref.1, bf16[16,8,128,128]{3,2,1,0:T(8,128)(2,1)} %right_ref.1, bf16[8,4,128,128]{3,2,1,0:T(8,128)(2,1)} %wave_ref.3), custom_call_target="tpu_custom_call" | custom-call | tf_op jit(solution)/shard_map/exchange/pallas_call | solution.py:139
  280.3 0.0 copy-start.2
  280.3 2.2 copy-done.2
  282.5 0.0 copy-start.3
  282.5 2.2 copy-done.3
  284.7 0.0 copy-start.4
  284.7 0.0 copy-start.5
  284.7 29.4 %products.1.sums_ref = f32[4,8,4,128,128]{4,3,2,1,0:T(8,128)S(1)} custom-call(s32[128]{0:T(128)S(1)} %reshape.24.pairs_ref, s32[32]{0:T(128)S(1)} %fusion.1.rows_ref, s32[128]{0:T(128)S(1)} %select_n.44.cols_ref, bf16[4,4,8,128,128]{4,3,2,1,0:T(8,128)(2,1)S(1)} %copy-done.2, bf16[4,8,4,128,128]{4,3,2,1,0:T(8,128)(2,1)S(1)} %copy-done.3, ...), custom_call_target="tpu_custom_call" | custom-call | flops 4294967296 | bytes 29360128 | tf_op jit(solution)/shard_map/products/pallas_call | solution.py:194
  314.1 0.0 copy-start.1
  314.1 3.2 copy-done.1
  317.3 0.0 copy-done.4
  317.3 0.0 copy-done.5
  317.3 35.3 %finish.1 = (bf16[8,4,128,128]{3,2,1,0:T(8,128)(2,1)S(1)}, f32[8,4,128,128]{3,2,1,0:T(8,128)S(1)}) custom-call(s32[8]{0:T(128)S(1)} %fusion.rows_ref, s32[32]{0:T(128)S(1)} %reshape.23.cols_ref, f32[4,8,4,128,128]{4,3,2,1,0:T(8,128)} %copy-done.1, bf16[8,4,128,128]{3,2,1,0:T(8,128)(2,1)S(1)} %copy-done.4, f32[8,4,128,128]{3,2,1,0:T(8,128)S(1)} %copy-done.5), custom_call_target="tpu_custom_call" | custom-call | tf_op jit(solution)/shard_map/finish/pallas_call | solution.py:330
  352.6 1.0 copy.13
  353.6 1.3 copy.14
  (4 shorter events, 0.0 us)
Async XLA Ops:
  0.6 1.0 copy-start
  280.3 2.2 copy-start.2
  282.5 2.2 copy-start.3
  284.7 32.6 %copy-start.4 = (bf16[8,4,128,128]{3,2,1,0:T(8,128)(2,1)S(1)}, bf16[8,4,128,128]{3,2,1,0:T(8,128)(2,1)}, u32[]{:S(2)}) copy-start(bf16[8,4,128,128]{3,2,1,0:T(8,128)(2,1)} %wave_ref.3) | copy-start | bytes 3145732
  284.7 32.6 %copy-start.5 = (f32[8,4,128,128]{3,2,1,0:T(8,128)S(1)}, f32[8,4,128,128]{3,2,1,0:T(8,128)}, u32[]{:S(2)}) copy-start(f32[8,4,128,128]{3,2,1,0:T(8,128)} %energy_ref.1) | copy-start | bytes 6291460
  314.1 3.2 copy-start.1

commit v3 on v2

--- a/solution.py
+++ b/solution.py
@@ -156,58 +156,65 @@
     )(left_env, right_env, wave)
 
 
-def products_kernel(partners, terms, pairs_ref, rows_ref, cols_ref, left_ref, wave_ref, *rest):
-    right_refs, out_ref = rest[:partners], rest[partners]
+GROUP = 4
+
+
+def products_kernel(group, partners, terms, pairs_ref, rows_ref, cols_ref, left_ref, wave_ref, *rest):
+    right_refs, out_ref = rest[:group * partners], rest[group * partners]
     size = wave_ref.shape[-1]
     step = pl.program_id(0)
     row_ids = lax.broadcasted_iota(jnp.int32, (size, size), 0)
     col_ids = lax.broadcasted_iota(jnp.int32, (size, size), 1)
-    masked = []
-    for k in range(partners):
-        live = (row_ids < rows_ref[step]) & (col_ids < cols_ref[step * partners + k])
-        masked.append(jnp.where(live, wave_ref[0, 0, k], jnp.zeros((), wave_ref.dtype)))
-    masked = jnp.concatenate(masked, axis=1)
-    halves = [jnp.dot(left_ref[0, w, 0], masked, preferred_element_type=jnp.float32).astype(jnp.bfloat16)
-              for w in range(terms)]
-    for k in range(partners):
-        first = jnp.concatenate([p[:, k * size:(k + 1) * size] for p in halves], axis=1)
-        second = jnp.concatenate([right_refs[k][0, w, 0] for w in range(terms)], axis=1)
-        out_ref[0, 0, k] = lax.dot_general(
-            first, second, (((1,), (1,)), ((), ())), preferred_element_type=jnp.float32
-        ).astype(out_ref.dtype)
+    for g in range(group):
+        sector = step * group + g
+        masked = []
+        for k in range(partners):
+            live = (row_ids < rows_ref[sector]) & (col_ids < cols_ref[sector * partners + k])
+            masked.append(jnp.where(live, wave_ref[0, g, k], jnp.zeros((), wave_ref.dtype)))
+        masked = jnp.concatenate(masked, axis=1)
+        left = left_ref[0, :, g].reshape(terms * size, size)
+        halves = jnp.dot(left, masked, preferred_element_type=jnp.float32).astype(jnp.bfloat16)
+        for k in range(partners):
+            first = jnp.concatenate(
+                [halves[w * size:(w + 1) * size, k * size:(k + 1) * size] for w in range(terms)], axis=1)
+            second = jnp.concatenate([right_refs[g * partners + k][0, w, 0] for w in range(terms)], axis=1)
+            out_ref[0, g, k] = lax.dot_general(
+                first, second, (((1,), (1,)), ((), ())), preferred_element_type=jnp.float32)
 
 
 def products(pairs, rows, cols, left_all, right_all, wave_all):
     team, sectors, partners, size, _ = wave_all.shape
     terms = left_all.shape[1]
-
-    def pick(k):
+    group = GROUP if sectors % GROUP == 0 else 1
+    steps = sectors // group
+
+    def pick(g, k):
         def index(i, pairs_ref, rows_ref, cols_ref):
-            b = pairs_ref[i * partners + k]
+            b = pairs_ref[(i * group + g) * partners + k]
             return (b // sectors, 0, b % sectors, 0, 0)
         return pl.BlockSpec((1, terms, 1, size, size), index)
 
     def own(i, *_):
-        return (i // sectors, i % sectors, 0, 0, 0)
+        return (i // steps, i % steps, 0, 0, 0)
 
     blocks = team * sectors * partners
     return pl.pallas_call(
-        functools.partial(products_kernel, partners, terms),
+        functools.partial(products_kernel, group, partners, terms),
         grid_spec=pltpu.PrefetchScalarGridSpec(
             num_scalar_prefetch=3,
-            grid=(team * sectors,),
+            grid=(team * steps,),
             in_specs=[
-                pl.BlockSpec((1, terms, 1, size, size), lambda i, *_: (i // sectors, 0, i % sectors, 0, 0)),
-                pl.BlockSpec((1, 1, partners, size, size), own),
-            ] + [pick(k) for k in range(partners)],
-            out_specs=pl.BlockSpec((1, 1, partners, size, size), own),
+                pl.BlockSpec((1, terms, group, size, size), lambda i, *_: (i // steps, 0, i % steps, 0, 0)),
+                pl.BlockSpec((1, group, partners, size, size), own),
+            ] + [pick(g, k) for g in range(group) for k in range(partners)],
+            out_specs=pl.BlockSpec((1, group, partners, size, size), own),
         ),
         out_shape=jax.ShapeDtypeStruct(wave_all.shape, jnp.float32),
-        compiler_params=pltpu.CompilerParams(vmem_limit_bytes=32 * 1024 * 1024),
+        compiler_params=pltpu.CompilerParams(vmem_limit_bytes=40 * 1024 * 1024),
         cost_estimate=pl.CostEstimate(flops=4 * blocks * terms * size ** 3,
-                                      bytes_accessed=28 * 2 ** 20, transcendentals=0),
+                                      bytes_accessed=32 * 2 ** 20, transcendentals=0),
         name="products",
-    )(pairs, rows, cols, left_all, wave_all, *([right_all] * partners))
+    )(pairs, rows, cols, left_all, wave_all, *([right_all] * (group * partners)))
 
 
 def finish_kernel(peers, rows_ref, cols_ref, sums_ref, wave_ref, energy_ref, sigma_ref, correction_ref,

time: 356 us -> 345 us (0.969)
  Pallas kernels: 341 us -> 334 us
    pallas_call x1, Pallas kernels: 29.4 us -> 22.2 us  [products(): pl.pallas_call(functools.partial(products_kernel, group, partners, terms)...]
    unnamed x15 -> x13, local copies, waits for them, and re-layouts: 9.99 us -> 6.77 us
where the time goes in v3:
time: 345 us
  Pallas kernels  334 us (97%)
  local copies, waits for them, and re-layouts  9.46 us (3%)
    pallas_call x1, Pallas kernels, exchange(): pl.pallas_call(functools.partial(exchange_kernel, lines, terms), out_shap...  277 us
    pallas_call x1, Pallas kernels, finish(): pl.pallas_call(functools.partial(finish_kernel, peers), out_shape=(jax.Sh...  35.3 us
    pallas_call x1, Pallas kernels, products(): pl.pallas_call(functools.partial(products_kernel, group, partners, terms)...  22.2 us

profile of v3, /device:TPU:0, one launch (start us, length us, event | category | flops | bytes accessed | tf_op | source)
XLA Modules:
  0.0 344.5 jit_solution(10133445212432248151)
XLA Ops:
  0.6 0.0 copy-start
  0.7 0.8 slice_bitcast_fusion
  1.4 0.1 fusion.rows_ref
  1.5 0.1 fusion.1.rows_ref
  1.6 0.0 copy-done
  1.6 0.1 constant_dynamic-slice_fusion.2
  1.7 0.1 copy.10
  1.8 0.1 reshape.24.pairs_ref
  1.9 0.1 reshape.27
  2.0 1.2 gather_fusion
  3.2 0.1 reshape.26
  3.3 0.1 select_n.44.cols_ref
  3.5 0.1 reshape.23.cols_ref
  3.5 276.8 %exchange.1 = (bf16[4,4,8,128,128]{4,3,2,1,0:T(8,128)(2,1)}, bf16[16,4,8,128,128]{4,3,2,1,0:T(8,128)(2,1)}, bf16[4,8,4,128,128]{4,3,2,1,0:T(8,128)(2,1)}) custom-call(bf16[16,8,128,128]{3,2,1,0:T(8,128)(2,1)} %left_ref.1, bf16[16,8,128,128]{3,2,1,0:T(8,128)(2,1)} %right_ref.1, bf16[8,4,128,128]{3,2,1,0:T(8,128)(2,1)} %wave_ref.3), custom_call_target="tpu_custom_call" | custom-call | tf_op jit(solution)/shard_map/exchange/pallas_call | solution.py:139
  280.3 0.0 copy-start.1
  280.3 2.2 copy-done.1
  282.5 0.0 copy-start.2
  282.5 2.2 copy-done.2
  284.7 0.0 copy-start.3
  284.7 0.0 copy-start.4
  284.7 22.2 %products.1.sums_ref = f32[4,8,4,128,128]{4,3,2,1,0:T(8,128)} custom-call(s32[128]{0:T(128)S(1)} %reshape.24.pairs_ref, s32[32]{0:T(128)S(1)} %fusion.1.rows_ref, s32[128]{0:T(128)S(1)} %select_n.44.cols_ref, bf16[4,4,8,128,128]{4,3,2,1,0:T(8,128)(2,1)S(1)} %copy-done.1, bf16[4,8,4,128,128]{4,3,2,1,0:T(8,128)(2,1)S(1)} %copy-done.2, ...), custom_call_target="tpu_custom_call" | custom-call | flops 4294967296 | bytes 33554432 | tf_op jit(solution)/shard_map/products/pallas_call | solution.py:201
  306.9 0.0 copy-done.3
  306.9 0.0 copy-done.4
  306.9 35.3 %finish.1 = (bf16[8,4,128,128]{3,2,1,0:T(8,128)(2,1)S(1)}, f32[8,4,128,128]{3,2,1,0:T(8,128)S(1)}) custom-call(s32[8]{0:T(128)S(1)} %fusion.rows_ref, s32[32]{0:T(128)S(1)} %reshape.23.cols_ref, f32[4,8,4,128,128]{4,3,2,1,0:T(8,128)} %products.1.sums_ref, bf16[8,4,128,128]{3,2,1,0:T(8,128)(2,1)S(1)} %copy-done.3, f32[8,4,128,128]{3,2,1,0:T(8,128)S(1)} %copy-done.4), custom_call_target="tpu_custom_call" | custom-call | tf_op jit(solution)/shard_map/finish/pallas_call | solution.py:337
  342.2 1.0 copy.13
  343.2 1.3 copy.14
  (4 shorter events, 0.0 us)
Async XLA Ops:
  0.6 1.0 copy-start
  280.3 2.2 copy-start.1
  282.5 2.2 copy-start.2
  284.7 22.2 %copy-start.3 = (bf16[8,4,128,128]{3,2,1,0:T(8,128)(2,1)S(1)}, bf16[8,4,128,128]{3,2,1,0:T(8,128)(2,1)}, u32[]{:S(2)}) copy-start(bf16[8,4,128,128]{3,2,1,0:T(8,128)(2,1)} %wave_ref.3) | copy-start | bytes 3145732
  284.7 22.2 %copy-start.4 = (f32[8,4,128,128]{3,2,1,0:T(8,128)S(1)}, f32[8,4,128,128]{3,2,1,0:T(8,128)}, u32[]{:S(2)}) copy-start(f32[8,4,128,128]{3,2,1,0:T(8,128)} %energy_ref.1) | copy-start | bytes 6291460

commit v4 on v3

--- a/solution.py
+++ b/solution.py
@@ -7,7 +7,7 @@
 from jax.sharding import PartitionSpec as P
 
 TEAM = 4
-PARTS = 2
+PARTS = 4
 
 
 def exchange_kernel(lines, terms, left_ref, right_ref, wave_ref, left_all, right_all, wave_all,

time: 345 us -> 346 us (level)
  no operation moved by 1% of the time
where the time goes in v4:
time: 346 us
  Pallas kernels  335 us (97%)
  local copies, waits for them, and re-layouts  9.46 us (3%)
    pallas_call x1, Pallas kernels, exchange(): pl.pallas_call(functools.partial(exchange_kernel, lines, terms), out_shap...  278 us
    pallas_call x1, Pallas kernels, finish(): pl.pallas_call(functools.partial(finish_kernel, peers), out_shape=(jax.Sh...  35.3 us
    pallas_call x1, Pallas kernels, products(): pl.pallas_call(functools.partial(products_kernel, group, partners, terms)...  22.2 us

profile of v4, /device:TPU:0, one launch (start us, length us, event | category | flops | bytes accessed | tf_op | source)
XLA Modules:
  0.0 345.5 jit_solution(18013193903049256523)
XLA Ops:
  0.6 0.0 copy-start
  0.7 0.8 slice_bitcast_fusion
  1.4 0.1 fusion.rows_ref
  1.5 0.1 fusion.1.rows_ref
  1.6 0.0 copy-done
  1.6 0.1 constant_dynamic-slice_fusion.2
  1.7 0.1 copy.10
  1.8 0.1 reshape.24.pairs_ref
  1.9 0.1 reshape.27
  2.0 1.2 gather_fusion
  3.2 0.1 reshape.26
  3.3 0.1 select_n.44.cols_ref
  3.5 0.1 reshape.23.cols_ref
  3.5 277.8 %exchange.1 = (bf16[4,4,8,128,128]{4,3,2,1,0:T(8,128)(2,1)}, bf16[16,4,8,128,128]{4,3,2,1,0:T(8,128)(2,1)}, bf16[4,8,4,128,128]{4,3,2,1,0:T(8,128)(2,1)}) custom-call(bf16[16,8,128,128]{3,2,1,0:T(8,128)(2,1)} %left_ref.1, bf16[16,8,128,128]{3,2,1,0:T(8,128)(2,1)} %right_ref.1, bf16[8,4,128,128]{3,2,1,0:T(8,128)(2,1)} %wave_ref.3), custom_call_target="tpu_custom_call" | custom-call | tf_op jit(solution)/shard_map/exchange/pallas_call | solution.py:139
  281.3 0.0 copy-start.1
  281.3 2.2 copy-done.1
  283.5 0.0 copy-start.2
  283.5 2.2 copy-done.2
  285.7 0.0 copy-start.3
  285.7 0.0 copy-start.4
  285.7 22.2 %products.1.sums_ref = f32[4,8,4,128,128]{4,3,2,1,0:T(8,128)} custom-call(s32[128]{0:T(128)S(1)} %reshape.24.pairs_ref, s32[32]{0:T(128)S(1)} %fusion.1.rows_ref, s32[128]{0:T(128)S(1)} %select_n.44.cols_ref, bf16[4,4,8,128,128]{4,3,2,1,0:T(8,128)(2,1)S(1)} %copy-done.1, bf16[4,8,4,128,128]{4,3,2,1,0:T(8,128)(2,1)S(1)} %copy-done.2, ...), custom_call_target="tpu_custom_call" | custom-call | flops 4294967296 | bytes 33554432 | tf_op jit(solution)/shard_map/products/pallas_call | solution.py:201
  307.9 0.0 copy-done.3
  307.9 0.0 copy-done.4
  307.9 35.3 %finish.1 = (bf16[8,4,128,128]{3,2,1,0:T(8,128)(2,1)S(1)}, f32[8,4,128,128]{3,2,1,0:T(8,128)S(1)}) custom-call(s32[8]{0:T(128)S(1)} %fusion.rows_ref, s32[32]{0:T(128)S(1)} %reshape.23.cols_ref, f32[4,8,4,128,128]{4,3,2,1,0:T(8,128)} %products.1.sums_ref, bf16[8,4,128,128]{3,2,1,0:T(8,128)(2,1)S(1)} %copy-done.3, f32[8,4,128,128]{3,2,1,0:T(8,128)S(1)} %copy-done.4), custom_call_target="tpu_custom_call" | custom-call | tf_op jit(solution)/shard_map/finish/pallas_call | solution.py:337
  343.2 1.0 copy.13
  344.2 1.3 copy.14
  (4 shorter events, 0.0 us)
Async XLA Ops:
  0.6 1.0 copy-start
  281.3 2.2 copy-start.1
  283.5 2.2 copy-start.2
  285.7 22.2 %copy-start.3 = (bf16[8,4,128,128]{3,2,1,0:T(8,128)(2,1)S(1)}, bf16[8,4,128,128]{3,2,1,0:T(8,128)(2,1)}, u32[]{:S(2)}) copy-start(bf16[8,4,128,128]{3,2,1,0:T(8,128)(2,1)} %wave_ref.3) | copy-start | bytes 3145732
  285.7 22.2 %copy-start.4 = (f32[8,4,128,128]{3,2,1,0:T(8,128)S(1)}, f32[8,4,128,128]{3,2,1,0:T(8,128)}, u32[]{:S(2)}) copy-start(f32[8,4,128,128]{3,2,1,0:T(8,128)} %energy_ref.1) | copy-start | bytes 6291460
